TPU v7x, 512 devices: a whole 4x8x8 slice. The times are simulated.
512 devices in a mesh: slab: 64 (over x, z, core), filt: 8 (over y).
Axes of the slice: x: 4, y: 8, z: 8, core: 2. Of those that a mesh axis runs over, the one named last changes fastest.
Arguments:
- volume: bfloat16 [128, 128, 16, 256], P('slab', 'filt'), may hold values from -6 to 6
- weights: bfloat16 [3, 3, 3, 128, 256], replicated, may hold values from -0.109375 to 0.109375
- out_error: bfloat16 [64, 256, 8, 128], P('slab', 'filt'), may hold values from -6 to 6
Outputs:
- in_grad: bfloat16 [128, 128, 16, 256], P('slab', None, 'filt')
- weight_grad: float32 [3, 3, 3, 128, 256], P(None, None, None, None, 'filt')
All inputs are finite; a program needn't handle non-finite values.
Results may differ from a plain program's by a relative error of at most 0.0049.
Values may be sent and summed in bfloat16 or wider, within the bound.
No kernel may reach another device: no remote copies, remote signals or barrier semaphores. Data moves between devices by JAX's collectives and lax.ppermute only.
A program may use at most 64 MiB of HBM per device.

v0:
```python
import math
import jax
import jax.numpy as jnp
from jax import lax
from jax.sharding import PartitionSpec as P


def shifted_2(value, axis, steps):
    count = lax.axis_size(axis)
    first, last = (max(0, -steps), min(count, count - steps))
    return lax.ppermute(value, axis, [(source, source + steps) for source in range(first, last)])


def tap_pieces(extended, top):
    depth = (extended.shape[0] - 1) // 2
    rows = (extended.shape[2] + top - 1) // 2
    cols = extended.shape[3] // 2
    chans = extended.shape[1]
    padded = jnp.pad(extended, ((0, 1), (0, 0), (top, 1), (1, 1)))
    split = padded.reshape(depth + 1, 2, chans, rows + 1, 2, cols + 1, 2)
    pieces = []
    for a in range(3):
        for b in range(3):
            for c in range(3):
                piece = split[
                    a // 2 : a // 2 + depth,
                    a % 2,
                    :,
                    b // 2 : b // 2 + rows,
                    b % 2,
                    c // 2 : c // 2 + cols,
                    c % 2,
                ]
                pieces.append(((a, b, c), piece))
    return pieces


def forward_taps(pieces, kernel):
    total = None
    for (a, b, c), piece in pieces:
        term = jnp.einsum(
            "dkhw,kf->dfhw", piece, kernel[a, b, c], preferred_element_type=jnp.float32
        )
        total = term if total is None else total + term
    return total


def weight_taps(pieces, grad):
    terms = []
    for (a, b, c), piece in pieces:
        terms.append(jnp.einsum("dkhw,dfhw->kf", piece, grad, preferred_element_type=jnp.float32))
    stacked = jnp.stack(terms, 0)
    return stacked.reshape((3, 3, 3) + stacked.shape[1:])


def input_taps(grad_ext, kernel):
    depth = grad_ext.shape[0] - 1
    rows = grad_ext.shape[2] - 1
    cols = grad_ext.shape[3]
    chans = kernel.shape[3]
    parity_taps = ((1,), (2, 0))
    shifted = {}
    for a in range(3):
        for b in range(3):
            for c in range(3):
                term = jnp.einsum(
                    "dfhw,kf->dkhw", grad_ext, kernel[a, b, c], preferred_element_type=jnp.float32
                )
                start_d = 1 if a == 0 else 0
                start_r = 1 if b == 0 else 0
                term = term[start_d : start_d + depth, :, start_r : start_r + rows]
                if c == 0:
                    term = jnp.pad(term[..., 1:], ((0, 0), (0, 0), (0, 0), (0, 1)))
                shifted[a, b, c] = term
    depth_parts = []
    for even_d in range(2):
        row_parts = []
        for even_r in range(2):
            col_parts = []
            for even_c in range(2):
                total = None
                for a in parity_taps[even_d]:
                    for b in parity_taps[even_r]:
                        for c in parity_taps[even_c]:
                            total = shifted[a, b, c] if total is None else total + shifted[a, b, c]
                col_parts.append(total)
            row_parts.append(jnp.stack(col_parts, -1))
        row_parts = jnp.stack(row_parts, 3)
        depth_parts.append(row_parts)
    joined = jnp.stack(depth_parts, 1)
    return joined.reshape(2 * depth, chans, 2 * rows, 2 * cols)


def activation_grad(preact, error):
    sigma = jax.nn.sigmoid(preact)
    return (error * (sigma * (1.0 + preact * (1.0 - sigma)))).astype(jnp.bfloat16)


def on_device(volume, weights, out_error):
    member = lax.axis_index("filt")
    tile = out_error.shape[1]
    below = shifted_2(volume[-1:], "slab", 1)
    extended = jnp.concatenate([below, volume], 0)
    whole = lax.all_gather(extended, "filt", axis=1, tiled=True)
    pieces = tap_pieces(whole, 1)
    kernel_tile = lax.dynamic_slice_in_dim(weights, member * tile, tile, 4)
    preact = forward_taps(pieces, kernel_tile)
    grad = activation_grad(preact, out_error)
    weight_part = weight_taps(pieces, grad)
    grad_rows = lax.all_to_all(grad, "filt", split_axis=2, concat_axis=1, tiled=True)
    count = out_error.shape[0] * lax.axis_size("slab") * out_error.shape[2] * out_error.shape[3]
    weight_grad = lax.psum(weight_part, "slab") * (1.0 / math.sqrt(count))
    upper = shifted_2(grad_rows, "slab", -1)
    grad_ext = jnp.concatenate([grad_rows, upper], 0)
    right_row = shifted_2(grad_ext, "filt", -1)
    grad_ext = jnp.concatenate([grad_ext, right_row], 2)
    in_grad = input_taps(grad_ext, weights).astype(jnp.bfloat16)
    return (in_grad, weight_grad)


def solution(mesh):
    in_specs = (P("slab", "filt", None, None), P(), P("slab", "filt", None, None))
    out_specs = (P("slab", None, "filt", None), P(None, None, None, None, "filt"))
    return jax.shard_map(
        on_device, mesh=mesh, in_specs=in_specs, out_specs=out_specs, check_vma=False
    )
```

profile of v0, /device:TPU:1, one launch (start us, length us, event | category | flops | bytes accessed | tf_op | source)
XLA Modules:
  0.0 422.1 jit_solution(12113445541933201036)
XLA Ops:
  8.1 5.4 %collective-permute-start = (bf16[1,16,16,256]{3,2,1,0:T(8,128)(2,1)S(1)}, bf16[1,16,16,256]{3,2,1,0:T(8,128)(2,1)S(1)}, u32[]{:S(2)}, u32[]{:S(2)}) collective-permute-start(bf16[1,16,16,256]{3,2,1,0:T(8,128)(2,1)S(1)} %slice.347), channel_id=1, source_target_pairs={{0,8},{8,16},{16,24},{24,32},{32,40},{40,48},{48,56},{56,64},{64,7... | collective-permute-start | bytes 393224 | tf_op jit(solution)/shard_map/ppermute | solution.py:11
  13.5 3.6 collective-permute-done
  18.9 51.0 %all-gather.2.cloned.1.call-done = bf16[3,128,16,256]{3,2,1,0:T(8,128)(2,1)} async-done(((bf16[3,16,16,256]{3,2,1,0:T(8,128)(2,1)}), bf16[3,128,16,256]{3,2,1,0:T(8,128)(2,1)}) %all-gather.2.cloned.1.call-update) | async-done | bytes 3145744 | tf_op jit(solution)/shard_map/all_gather | solution.py:104
  69.9 6.1 %copy.203 = bf16[3,128,16,256]{1,0,3,2:T(4,128)(2,1)} copy(bf16[3,128,16,256]{3,2,1,0:T(8,128)(2,1)} %all-gather.2.cloned.1.call-done) | data formatting | bytes 6291456
  76.0 3.9 pad.32.clone
  79.9 4.1 fusion.214
  84.0 11.3 %fusion.213 = (bf16[1,1,128,8,1,128,1]{2,1,0,6,5,4,3:T(2,128)(2,1)}, bf16[1,1,128,8,1,128,1]{2,1,0,6,5,4,3:T(2,128)(2,1)}, bf16[1,1,128,8,1,128,1]{2,1,0,6,5,4,3...) fusion(bf16[2,2,128,9,2,129,2]{2,1,0,6,5,4,3:T(2,128)(2,1)S(1)}, ...), kind=kLoop, calls=%fused_computation.343 | loop fusion | bytes 9961472 | tf_op jit(solution)/shard_map/slice | solution.py:25
  97.4 1.9 copy.158
  101.2 1.9 copy.154
  103.0 1.9 copy.152
  104.9 1.9 copy.150
  106.8 1.9 copy.202
  118.8 1.9 copy.180
  120.7 1.9 copy.178
  122.6 1.9 copy.176
  124.5 1.9 copy.174
  126.3 1.9 copy.172
  128.2 1.9 copy.170
  130.1 1.9 copy.168
  132.0 1.9 copy.166
  165.6 4.6 %all-to-all-start = ((bf16[1,32,8,128]{3,1,0,2:T(8,128)(2,1)}), bf16[1,32,8,128]{3,1,0,2:T(8,128)(2,1)S(1)}, u32[]{:S(2)}, u32[]{:S(2)}) async-start(bf16[1,32,8,128]{3,1,0,2:T(8,128)(2,1)} %bitcast.83), calls=%async_computation | async-start | bytes 131072 | tf_op jit(solution)/shard_map/all_to_all | solution.py:110
  214.3 3.0 collective-permute-start.1
  217.3 3.2 collective-permute-done.1
  221.8 183.9 %all-reduce.12.cloned.1.call-done = f32[3,3,3,128,32]{3,4,2,1,0:T(8,128)} async-done(((f32[3,3,3,128,32]{3,4,2,1,0:T(8,128)}), f32[3,3,3,128,32]{3,4,2,1,0:T(8,128)}) %all-reduce.12.cloned.1.call-update) | async-done | bytes 442384 | tf_op jit(solution)/shard_map/psum | solution.py:112
  (175 shorter events, 102.6 us)
Async XLA Ops:
  7.2 62.7 %all-gather.2.cloned.1.call-start = ((), (), s32[]{:S(2)}) async-start(), calls=%async_computation.1 | async-start | bytes 3538944 | tf_op jit(solution)/shard_map/all_gather | solution.py:104
  8.1 9.0 %collective-permute-start = (bf16[1,16,16,256]{3,2,1,0:T(8,128)(2,1)S(1)}, bf16[1,16,16,256]{3,2,1,0:T(8,128)(2,1)S(1)}, u32[]{:S(2)}, u32[]{:S(2)}) collective-permute-start(bf16[1,16,16,256]{3,2,1,0:T(8,128)(2,1)S(1)} %slice.347), channel_id=1, source_target_pairs={{0,8},{8,16},{16,24},{24,32},{32,40},{40,48},{48,56},{56,64},{64,7... | collective-permute-start | bytes 393224 | tf_op jit(solution)/shard_map/ppermute | solution.py:11
  136.4 7.0 %copy-start.16 = (bf16[1,1,128,8,1,128,1]{5,2,3,6,4,1,0:T(8,128)(2,1)S(1)}, bf16[1,1,128,8,1,128,1]{5,2,3,6,4,1,0:T(8,128)(2,1)}, u32[]{:S(2)}) copy-start(bf16[1,1,128,8,1,128,1]{5,2,3,6,4,1,0:T(8,128)(2,1)} %copy.166) | copy-start | bytes 786436
  137.7 6.8 %copy-start.14 = (bf16[1,1,128,8,1,128,1]{5,2,3,6,4,1,0:T(8,128)(2,1)S(1)}, bf16[1,1,128,8,1,128,1]{5,2,3,6,4,1,0:T(8,128)(2,1)}, u32[]{:S(2)}) copy-start(bf16[1,1,128,8,1,128,1]{5,2,3,6,4,1,0:T(8,128)(2,1)} %copy.168) | copy-start | bytes 786436
  139.0 6.5 %copy-start.11 = (bf16[1,1,128,8,1,128,1]{5,2,3,6,4,1,0:T(8,128)(2,1)S(1)}, bf16[1,1,128,8,1,128,1]{5,2,3,6,4,1,0:T(8,128)(2,1)}, u32[]{:S(2)}) copy-start(bf16[1,1,128,8,1,128,1]{5,2,3,6,4,1,0:T(8,128)(2,1)} %copy.170) | copy-start | bytes 786436
  140.1 6.5 %copy-start.9 = (bf16[1,1,128,8,1,128,1]{5,2,3,6,4,1,0:T(8,128)(2,1)S(1)}, bf16[1,1,128,8,1,128,1]{5,2,3,6,4,1,0:T(8,128)(2,1)}, u32[]{:S(2)}) copy-start(bf16[1,1,128,8,1,128,1]{5,2,3,6,4,1,0:T(8,128)(2,1)} %copy.172) | copy-start | bytes 786436
  141.1 6.5 %copy-start.7 = (bf16[1,1,128,8,1,128,1]{5,2,3,6,4,1,0:T(8,128)(2,1)S(1)}, bf16[1,1,128,8,1,128,1]{5,2,3,6,4,1,0:T(8,128)(2,1)}, u32[]{:S(2)}) copy-start(bf16[1,1,128,8,1,128,1]{5,2,3,6,4,1,0:T(8,128)(2,1)} %copy.174) | copy-start | bytes 786436
  142.2 6.4 %copy-start.5 = (bf16[1,1,128,8,1,128,1]{5,2,3,6,4,1,0:T(8,128)(2,1)S(1)}, bf16[1,1,128,8,1,128,1]{5,2,3,6,4,1,0:T(8,128)(2,1)}, u32[]{:S(2)}) copy-start(bf16[1,1,128,8,1,128,1]{5,2,3,6,4,1,0:T(8,128)(2,1)} %copy.176) | copy-start | bytes 786436
  143.3 6.4 %copy-start.3 = (bf16[1,1,128,8,1,128,1]{5,2,3,6,4,1,0:T(8,128)(2,1)S(1)}, bf16[1,1,128,8,1,128,1]{5,2,3,6,4,1,0:T(8,128)(2,1)}, u32[]{:S(2)}) copy-start(bf16[1,1,128,8,1,128,1]{5,2,3,6,4,1,0:T(8,128)(2,1)} %copy.178) | copy-start | bytes 786436
  157.0 7.0 %copy-start.13 = (bf16[1,1,128,8,1,128,1]{5,2,3,6,4,1,0:T(8,128)(2,1)S(1)}, bf16[1,1,128,8,1,128,1]{5,2,3,6,4,1,0:T(8,128)(2,1)}, u32[]{:S(2)}) copy-start(bf16[1,1,128,8,1,128,1]{5,2,3,6,4,1,0:T(8,128)(2,1)} %copy.150) | copy-start | bytes 786436
  165.6 48.6 %all-to-all-start = ((bf16[1,32,8,128]{3,1,0,2:T(8,128)(2,1)}), bf16[1,32,8,128]{3,1,0,2:T(8,128)(2,1)S(1)}, u32[]{:S(2)}, u32[]{:S(2)}) async-start(bf16[1,32,8,128]{3,1,0,2:T(8,128)(2,1)} %bitcast.83), calls=%async_computation | async-start | bytes 131072 | tf_op jit(solution)/shard_map/all_to_all | solution.py:110
  170.3 235.4 %all-reduce.12.cloned.1.call-start = ((), (), s32[]{:S(2)}) async-start(), calls=%async_computation.2 | async-start | bytes 884736 | tf_op jit(solution)/shard_map/psum | solution.py:112
  170.5 12.3 %copy-start.17 = (bf16[1,1,128,8,1,128,1]{5,2,3,6,4,1,0:T(8,128)(2,1)S(1)}, bf16[1,1,128,8,1,128,1]{5,2,3,6,4,1,0:T(8,128)(2,1)}, u32[]{:S(2)}) copy-start(bf16[1,1,128,8,1,128,1]{5,2,3,6,4,1,0:T(8,128)(2,1)} %copy.166) | copy-start | bytes 786436
  170.5 13.9 %copy-start.15 = (bf16[1,1,128,8,1,128,1]{5,2,3,6,4,1,0:T(8,128)(2,1)S(1)}, bf16[1,1,128,8,1,128,1]{5,2,3,6,4,1,0:T(8,128)(2,1)}, u32[]{:S(2)}) copy-start(bf16[1,1,128,8,1,128,1]{5,2,3,6,4,1,0:T(8,128)(2,1)} %copy.168) | copy-start | bytes 786436
  170.5 15.5 %copy-start.12 = (bf16[1,1,128,8,1,128,1]{5,2,3,6,4,1,0:T(8,128)(2,1)S(1)}, bf16[1,1,128,8,1,128,1]{5,2,3,6,4,1,0:T(8,128)(2,1)}, u32[]{:S(2)}) copy-start(bf16[1,1,128,8,1,128,1]{5,2,3,6,4,1,0:T(8,128)(2,1)} %copy.170) | copy-start | bytes 786436
  170.5 17.2 %copy-start.10 = (bf16[1,1,128,8,1,128,1]{5,2,3,6,4,1,0:T(8,128)(2,1)S(1)}, bf16[1,1,128,8,1,128,1]{5,2,3,6,4,1,0:T(8,128)(2,1)}, u32[]{:S(2)}) copy-start(bf16[1,1,128,8,1,128,1]{5,2,3,6,4,1,0:T(8,128)(2,1)} %copy.172) | copy-start | bytes 786436
  172.4 17.0 %copy-start.8 = (bf16[1,1,128,8,1,128,1]{5,2,3,6,4,1,0:T(8,128)(2,1)S(1)}, bf16[1,1,128,8,1,128,1]{5,2,3,6,4,1,0:T(8,128)(2,1)}, u32[]{:S(2)}) copy-start(bf16[1,1,128,8,1,128,1]{5,2,3,6,4,1,0:T(8,128)(2,1)} %copy.174) | copy-start | bytes 786436
  174.2 16.8 %copy-start.6 = (bf16[1,1,128,8,1,128,1]{5,2,3,6,4,1,0:T(8,128)(2,1)S(1)}, bf16[1,1,128,8,1,128,1]{5,2,3,6,4,1,0:T(8,128)(2,1)}, u32[]{:S(2)}) copy-start(bf16[1,1,128,8,1,128,1]{5,2,3,6,4,1,0:T(8,128)(2,1)} %copy.176) | copy-start | bytes 786436
  176.0 16.7 %copy-start.4 = (bf16[1,1,128,8,1,128,1]{5,2,3,6,4,1,0:T(8,128)(2,1)S(1)}, bf16[1,1,128,8,1,128,1]{5,2,3,6,4,1,0:T(8,128)(2,1)}, u32[]{:S(2)}) copy-start(bf16[1,1,128,8,1,128,1]{5,2,3,6,4,1,0:T(8,128)(2,1)} %copy.178) | copy-start | bytes 786436
  177.8 16.5 %copy-start.2 = (bf16[1,1,128,8,1,128,1]{5,2,3,6,4,1,0:T(8,128)(2,1)S(1)}, bf16[1,1,128,8,1,128,1]{5,2,3,6,4,1,0:T(8,128)(2,1)}, u32[]{:S(2)}) copy-start(bf16[1,1,128,8,1,128,1]{5,2,3,6,4,1,0:T(8,128)(2,1)} %copy.180) | copy-start | bytes 786436
  195.9 16.6 %copy-start.19 = (bf16[1,1,128,8,1,128,1]{5,2,3,6,4,1,0:T(8,128)(2,1)S(1)}, bf16[1,1,128,8,1,128,1]{5,2,3,6,4,1,0:T(8,128)(2,1)}, u32[]{:S(2)}) copy-start(bf16[1,1,128,8,1,128,1]{5,2,3,6,4,1,0:T(8,128)(2,1)} %copy.202) | copy-start | bytes 786436
  207.5 200.0 %copy-start.20 = (bf16[3,3,3,128,256]{4,3,2,1,0:T(8,128)(2,1)S(1)}, bf16[3,3,3,128,256]{4,3,2,1,0:T(8,128)(2,1)}, u32[]{:S(2)}) copy-start(bf16[3,3,3,128,256]{4,3,2,1,0:T(8,128)(2,1)} %param.4) | copy-start | bytes 5308420
  214.3 6.1 %collective-permute-start.1 = (bf16[1,256,1,128]{1,3,2,0:T(8,128)(2,1)S(1)}, bf16[1,256,1,128]{1,3,2,0:T(8,128)(2,1)S(1)}, u32[]{:S(2)}, u32[]{:S(2)}) collective-permute-start(bf16[1,256,1,128]{1,3,2,0:T(8,128)(2,1)S(1)} %copy.115), channel_id=1, source_target_pairs={{8,0},{16,8},{24,16},{32,24},{40,32},{48,40},{56,48},{64,56},{72,6... | collective-permute-start | bytes 196616 | tf_op jit(solution)/shard_map/ppermute | solution.py:11
  220.5 187.0 %collective-permute-start.2 = (bf16[2,256,1,128]{1,3,2,0:T(8,128)(2,1)S(1)}, bf16[2,256,1,128]{1,3,2,0:T(8,128)(2,1)S(1)}, u32[]{:S(2)}, u32[]{:S(2)}) collective-permute-start(bf16[2,256,1,128]{1,3,2,0:T(8,128)(2,1)S(1)} %pad_maximum_fusion.2), channel_id=1, source_target_pairs={{1,0},{2,1},{3,2},{4,3},{5,4},{6,5},{7,6},{9,8},{10,9},{11,10},{12... | collective-permute-start | bytes 393224 | tf_op jit(solution)/shard_map/ppermute | solution.py:11
  (4 other events, 24.1 us)
Sparse Core Ops, SparseCore 0:
  19.0 50.8 all-gather.1
  214.3 191.2 all-reduce.11
where the time goes:
time: 425 us; the launch traced here: 422 us
  waiting for transfers between devices  242 us (57%)
  matrix products  80.7 us (19%)
  local copies, waits for them, and re-layouts  66.4 us (16%)
  between operations  15 us (4%)
  starting transfers between devices  14.5 us (3%)
    psum x1, waiting for transfers between devices, on_device(): weight_grad = lax.psum(weight_part, 'slab') * (1.0 / math.sqrt(count))  184 us
    all_gather x1, waiting for transfers between devices, on_device(): whole = lax.all_gather(extended, 'filt', axis=1, tiled=True)  51 us
    unnamed x73, local copies, waits for them, and re-layouts  45.6 us
    dot_general x27, matrix products, weight_taps(): jnp.einsum('dkhw,dfhw->kf', piece, grad, preferred_element_type=jnp.float32)  45.2 us
    dot_general x27, matrix products, forward_taps(): jnp.einsum('dkhw,kf->dfhw', piece, kernel[a, b, c], preferred_element_typ...  29.6 us
    slice x2, local copies, waits for them, and re-layouts, tap_pieces(): split[a // 2:a // 2 + depth, a % 2, :, b // 2:b // 2 + rows, b % 2, c //...  15.4 us
    ppermute x3, starting transfers between devices, shifted_2(): lax.ppermute(value, axis, [(source, source + steps) for source in range(f...  9.64 us
  transfers between devices with their start and end apart: 6, of which 4 were waited for; matrix products, arithmetic and copies ran while one was open for 11% of the time, Pallas kernels for 0%

commit v1 on v0

--- a/solution.py
+++ b/solution.py
@@ -3,6 +3,24 @@
 import jax.numpy as jnp
 from jax import lax
 from jax.sharding import PartitionSpec as P
+
+
+def gather_around(array, axis, dim):
+    ways, here, step = (lax.axis_size(axis), lax.axis_index(axis), array.shape[dim])
+    dims = [n * ways if d == dim else n for d, n in enumerate(array.shape)]
+    full = lax.dynamic_update_slice_in_dim(
+        jnp.zeros(dims, array.dtype), array, here * step, axis=dim
+    )
+    going_up = going_down = array
+    for far in range(1, ways // 2 + 1):
+        going_up = lax.ppermute(going_up, axis, [(d, (d + 1) % ways) for d in range(ways)])
+        full = lax.dynamic_update_slice_in_dim(full, going_up, (here - far) % ways * step, axis=dim)
+        if 2 * far < ways:
+            going_down = lax.ppermute(going_down, axis, [(d, (d - 1) % ways) for d in range(ways)])
+            full = lax.dynamic_update_slice_in_dim(
+                full, going_down, (here + far) % ways * step, axis=dim
+            )
+    return full
 
 
 def shifted_2(value, axis, steps):
@@ -101,7 +119,7 @@
     tile = out_error.shape[1]
     below = shifted_2(volume[-1:], "slab", 1)
     extended = jnp.concatenate([below, volume], 0)
-    whole = lax.all_gather(extended, "filt", axis=1, tiled=True)
+    whole = gather_around(extended, "filt", 1)
     pieces = tap_pieces(whole, 1)
     kernel_tile = lax.dynamic_slice_in_dim(weights, member * tile, tile, 4)
     preact = forward_taps(pieces, kernel_tile)

time: 425 us -> 5290 us (12.45)
  local copies, waits for them, and re-layouts: 66.4 us -> 4940 us
    dynamic_update_slice x0 -> x8, local copies, waits for them, and re-layouts: none -> 4850 us  [the longest x4 2700 us: gather_around(): lax.dynamic_update_slice_in_dim(full, going_up, (here - far) % ways * ste...]
  transfers between devices with their start and end apart: 6 -> 12, of which waited for: 4 -> 6; matrix products, arithmetic and copies ran while one was open for 11% -> 80% of each run, Pallas kernels for 0% -> 0%
where the time goes in v1:
time: 5290 us
  local copies, waits for them, and re-layouts  4940 us (93%)
  waiting for transfers between devices  214 us (4%)
  matrix products  80.8 us (2%)
    dynamic_update_slice x4, local copies, waits for them, and re-layouts, gather_around(): lax.dynamic_update_slice_in_dim(full, going_up, (here - far) % ways * ste...  2700 us
    dynamic_update_slice x3, local copies, waits for them, and re-layouts, gather_around(): lax.dynamic_update_slice_in_dim(full, going_down, (here + far) % ways * s...  2020 us
    psum x1, waiting for transfers between devices, on_device(): weight_grad = lax.psum(weight_part, 'slab') * (1.0 / math.sqrt(count))  186 us
    dynamic_update_slice x1, local copies, waits for them, and re-layouts, gather_around(): lax.dynamic_update_slice_in_dim(jnp.zeros(dims, array.dtype), array, here...  123 us
  transfers between devices with their start and end apart: 12, of which 6 were waited for; matrix products, arithmetic and copies ran while one was open for 80% of the time, Pallas kernels for 0%

profile of v1, /device:TPU:1, one launch (start us, length us, event | category | flops | bytes accessed | tf_op | source)
XLA Modules:
  0.0 5288.3 jit_solution(9816795602712230355)
XLA Ops:
  8.1 5.4 collective-permute-start
  13.5 3.6 collective-permute-done
  20.0 4.6 collective-permute-start.2
  24.6 7.2 collective-permute-done.1
  33.7 4.6 collective-permute-start.4
  38.2 6.2 collective-permute-done.3
  46.4 4.6 collective-permute-start.6
  51.0 5.3 collective-permute-done.5
  61.9 3.6 broadcast_in_dim.3
  65.5 123.1 %dynamic_update_slice.24 = bf16[3,128,16,256]{1,0,3,2:T(4,128)(2,1)} dynamic-update-slice(bf16[3,128,16,256]{1,0,3,2:T(4,128)(2,1)} %broadcast_in_dim.3, bf16[3,16,16,256]{1,0,3,2:T(4,128)(2,1)} %copy.99, s32[]{:T(128)} %constant.56.clone.1, s32[]{:T(128)S(6)} %select_n.59, s32[]{:T(128)} %constant.56.clone.1, s32[]{:T(128)} %constant.56.clone.1) | dynamic-update-slice | bytes 786436 | tf_op jit(solution)/shard_map/dynamic_update_slice | solution.py:11
  192.2 674.7 %dynamic_update_slice.25 = bf16[3,128,16,256]{1,0,3,2:T(4,128)(2,1)} dynamic-update-slice(bf16[3,128,16,256]{1,0,3,2:T(4,128)(2,1)} %dynamic_update_slice.24, bf16[3,16,16,256]{1,0,3,2:T(4,128)(2,1)} %copy.100, s32[]{:T(128)} %constant.56.clone.1, s32[]{:T(128)S(6)} %select_n.61, s32[]{:T(128)} %constant.56.clone.1, s32[]{:T(128)} %constant.56.clone.1) | dynamic-update-slice | bytes 786436 | tf_op jit(solution)/shard_map/dynamic_update_slice | solution.py:17
  870.4 674.7 %dynamic_update_slice.26 = bf16[3,128,16,256]{1,0,3,2:T(4,128)(2,1)} dynamic-update-slice(bf16[3,128,16,256]{1,0,3,2:T(4,128)(2,1)} %dynamic_update_slice.25, bf16[3,16,16,256]{1,0,3,2:T(4,128)(2,1)} %copy.101, s32[]{:T(128)} %constant.56.clone.1, s32[]{:T(128)S(6)} %select_n.63, s32[]{:T(128)} %constant.56.clone.1, s32[]{:T(128)} %constant.56.clone.1) | dynamic-update-slice | bytes 786436 | tf_op jit(solution)/shard_map/dynamic_update_slice | solution.py:20
  1548.7 674.7 %dynamic_update_slice.27 = bf16[3,128,16,256]{1,0,3,2:T(4,128)(2,1)} dynamic-update-slice(bf16[3,128,16,256]{1,0,3,2:T(4,128)(2,1)} %dynamic_update_slice.26, bf16[3,16,16,256]{1,0,3,2:T(4,128)(2,1)} %copy.102, s32[]{:T(128)} %constant.56.clone.1, s32[]{:T(128)S(6)} %select_n.65, s32[]{:T(128)} %constant.56.clone.1, s32[]{:T(128)} %constant.56.clone.1) | dynamic-update-slice | bytes 786436 | tf_op jit(solution)/shard_map/dynamic_update_slice | solution.py:17
  2227.0 674.7 %dynamic_update_slice.28 = bf16[3,128,16,256]{1,0,3,2:T(4,128)(2,1)} dynamic-update-slice(bf16[3,128,16,256]{1,0,3,2:T(4,128)(2,1)} %dynamic_update_slice.27, bf16[3,16,16,256]{1,0,3,2:T(4,128)(2,1)} %copy.103, s32[]{:T(128)} %constant.56.clone.1, s32[]{:T(128)S(6)} %select_n.67, s32[]{:T(128)} %constant.56.clone.1, s32[]{:T(128)} %constant.56.clone.1) | dynamic-update-slice | bytes 786436 | tf_op jit(solution)/shard_map/dynamic_update_slice | solution.py:20
  2905.3 674.7 %dynamic_update_slice.29 = bf16[3,128,16,256]{1,0,3,2:T(4,128)(2,1)} dynamic-update-slice(bf16[3,128,16,256]{1,0,3,2:T(4,128)(2,1)} %dynamic_update_slice.28, bf16[3,16,16,256]{1,0,3,2:T(4,128)(2,1)} %copy.104, s32[]{:T(128)} %constant.56.clone.1, s32[]{:T(128)S(6)} %select_n.69, s32[]{:T(128)} %constant.56.clone.1, s32[]{:T(128)} %constant.56.clone.1) | dynamic-update-slice | bytes 786436 | tf_op jit(solution)/shard_map/dynamic_update_slice | solution.py:17
  3583.6 674.7 %dynamic_update_slice.30 = bf16[3,128,16,256]{1,0,3,2:T(4,128)(2,1)} dynamic-update-slice(bf16[3,128,16,256]{1,0,3,2:T(4,128)(2,1)} %dynamic_update_slice.29, bf16[3,16,16,256]{1,0,3,2:T(4,128)(2,1)} %copy.105, s32[]{:T(128)} %constant.56.clone.1, s32[]{:T(128)S(6)} %select_n.71, s32[]{:T(128)} %constant.56.clone.1, s32[]{:T(128)} %constant.56.clone.1) | dynamic-update-slice | bytes 786436 | tf_op jit(solution)/shard_map/dynamic_update_slice | solution.py:20
  4261.8 674.9 %dynamic_update_slice.31 = bf16[3,128,16,256]{1,0,3,2:T(4,128)(2,1)} dynamic-update-slice(bf16[3,128,16,256]{1,0,3,2:T(4,128)(2,1)} %dynamic_update_slice.30, bf16[3,16,16,256]{1,0,3,2:T(4,128)(2,1)} %copy.106, s32[]{:T(128)} %constant.56.clone.1, s32[]{:T(128)S(6)} %select_n.73, s32[]{:T(128)} %constant.56.clone.1, s32[]{:T(128)} %constant.56.clone.1) | dynamic-update-slice | bytes 786436 | tf_op jit(solution)/shard_map/dynamic_update_slice | solution.py:17
  4936.8 4.0 pad.32
  4940.7 4.9 fusion.214
  4945.7 11.0 fusion.213
  5025.9 4.3 all-to-all-start
  5074.2 4.9 collective-permute-start.8
  5079.1 4.7 collective-permute-done.8
  5085.4 186.5 %all-reduce.12.cloned.1.call-done = f32[3,3,3,128,32]{3,4,2,1,0:T(8,128)} async-done(((f32[3,3,3,128,32]{3,4,2,1,0:T(8,128)}), f32[3,3,3,128,32]{3,4,2,1,0:T(8,128)}) %all-reduce.12.cloned.1.call-update) | async-done | bytes 442384 | tf_op jit(solution)/shard_map/psum | solution.py:130
  (199 shorter events, 161.2 us)
Async XLA Ops:
  8.1 9.0 collective-permute-start
  18.1 13.7 collective-permute-start.1
  20.0 13.7 collective-permute-start.2
  31.7 12.7 collective-permute-start.3
  33.7 12.7 collective-permute-start.4
  44.5 11.8 collective-permute-start.5
  46.4 3533.6 %collective-permute-start.6 = (bf16[3,16,16,256]{3,2,1,0:T(8,128)(2,1)S(1)}, bf16[3,16,16,256]{3,2,1,0:T(8,128)(2,1)S(1)}, u32[]{:S(2)}, u32[]{:S(2)}) collective-permute-start(bf16[3,16,16,256]{3,2,1,0:T(8,128)(2,1)S(1)} %collective-permute-done.4), channel_id=1, source_target_pairs={{0,7},{1,0},{2,1},{3,2},{4,3},{5,4},{6,5},{7,6},{8,15},{9,8},{10,9... | collective-permute-start | bytes 1179656 | tf_op jit(solution)/shard_map/ppermute | solution.py:19
  56.3 4202.0 %collective-permute-start.7 = (bf16[3,16,16,256]{3,2,1,0:T(8,128)(2,1)S(1)}, bf16[3,16,16,256]{3,2,1,0:T(8,128)(2,1)S(1)}, u32[]{:S(2)}, u32[]{:S(2)}) collective-permute-start(bf16[3,16,16,256]{3,2,1,0:T(8,128)(2,1)S(1)} %collective-permute-done.5), channel_id=1, source_target_pairs={{0,1},{1,2},{2,3},{3,4},{4,5},{5,6},{6,7},{7,0},{8,9},{9,10},{10,1... | collective-permute-start | bytes 1179656 | tf_op jit(solution)/shard_map/ppermute | solution.py:16
  4994.2 7.4 copy-start.10
  4995.5 7.2 copy-start.11
  4996.8 7.0 copy-start.8
  5017.3 7.0 copy-start.15
  5025.9 48.2 all-to-all-start
  5030.2 241.6 %all-reduce.12.cloned.1.call-start = ((), (), s32[]{:S(2)}) async-start(), calls=%async_computation.1 | async-start | bytes 884736 | tf_op jit(solution)/shard_map/psum | solution.py:130
  5030.3 10.7 copy-start.12
  5030.3 12.4 copy-start.9
  5030.3 14.0 copy-start.7
  5030.3 15.6 copy-start.5
  5030.3 17.3 copy-start.3
  5032.2 17.1 copy-start.1
  5055.8 16.6 copy-start.17
  5065.7 207.9 %copy-start.18 = (bf16[3,3,3,128,256]{4,3,2,1,0:T(8,128)(2,1)S(1)}, bf16[3,3,3,128,256]{4,3,2,1,0:T(8,128)(2,1)}, u32[]{:S(2)}) copy-start(bf16[3,3,3,128,256]{4,3,2,1,0:T(8,128)(2,1)} %param.4) | copy-start | bytes 5308420
  5074.2 9.6 collective-permute-start.8
  5083.8 189.8 %collective-permute-start.9 = (bf16[2,256,1,128]{1,3,2,0:T(8,128)(2,1)S(1)}, bf16[2,256,1,128]{1,3,2,0:T(8,128)(2,1)S(1)}, u32[]{:S(2)}, u32[]{:S(2)}) collective-permute-start(bf16[2,256,1,128]{1,3,2,0:T(8,128)(2,1)S(1)} %pad_maximum_fusion.1), channel_id=1, source_target_pairs={{1,0},{2,1},{3,2},{4,3},{5,4},{6,5},{7,6},{9,8},{10,9},{11,10},{12... | collective-permute-start | bytes 393224 | tf_op jit(solution)/shard_map/ppermute | solution.py:29
  (8 other events, 50.0 us)
Sparse Core Ops, SparseCore 0:
  5074.2 197.5 all-reduce.11
